TPU v7x, 32 devices: a whole 2x2x4 slice. The times are simulated.
32 devices in a mesh: vid: 4 (over z), ty: 2 (over y), tx: 4 (over x, core).
Axes of the slice: x: 2, y: 2, z: 4, core: 2. Of those that a mesh axis runs over, the one named last changes fastest.
Arguments:
- latent_shards: bfloat16 [4, 99328], P('vid', ('ty', 'tx')), may hold values from -6 to 6
- shard_starts: int32 [4, 9], P('vid'), may hold values from 0 to 4096, as said below
- frame_dims: int32 [4, 2], P('vid'), may hold values from 16 to 128, as said below
- latent_cache: bfloat16 [4, 2, 32, 2048], P('vid', None, 'ty', 'tx'), may hold values from -6 to 6
- feature_cache: bfloat16 [4, 2, 32, 49152], P('vid', None, 'ty', 'tx'), may hold values from -5 to 5
- in_weight: bfloat16 [432, 384], replicated, may hold values from -0.3125 to 0.3125
- in_bias: float32 [384], replicated, may hold values from -3 to 3
- norm_gain: float32 [384], replicated, may hold values from 0.1 to 1.9
- res_weight: bfloat16 [10368, 384], replicated, may hold values from -0.0625 to 0.0625
- res_bias: float32 [384], replicated, may hold values from -3 to 3
- up_weight: bfloat16 [3456, 192], replicated, may hold values from -0.109375 to 0.109375
- up_bias: float32 [192], replicated, may hold values from -3 to 3
Outputs:
- decoded: bfloat16 [4, 64, 49152], P('vid', 'ty', 'tx')
Inputs may be any that keep to these rules, and one draw needn't show every extreme that they name: `frame_dims`: row i gives video i's height, from 16 to 32, and width, from 64 to 128; one video fills the whole canvas and another is exactly 16 by 64. `shard_starts`: row i starts at 0, never falls, ends at video i's height times width, and every shard's token count fits its 776 slots; tokens lie in row-major order of the frame.
All inputs are finite; a program needn't handle non-finite values.
Results may differ from a plain program's by a relative error of at most 0.0095.
Values may be sent and summed in bfloat16 or wider, within the bound.
A program may use at most 64 MiB of HBM per device.

v0:
```python
import jax
import jax.numpy as jnp
from jax import lax
from jax.sharding import PartitionSpec as P

EPS = 1e-06


def padded_2(value, sides, width):
    for axis, dim in sides:
        size, length = (lax.axis_size(axis), value.shape[dim])
        up = [(i, (i + 1) % size) for i in range(size - 1)]
        down = [(j, i) for i, j in up]
        last = lax.slice_in_dim(value, length - width, length, axis=dim)
        leading = lax.slice_in_dim(value, 0, width, axis=dim)
        before = lax.ppermute(last, axis, up)
        after = lax.ppermute(leading, axis, down)
        value = jnp.concatenate([before, value, after], axis=dim)
    return value


def tap_sum(padded, weight, row_count, col_count):
    channels = padded.shape[-1]
    summed = jnp.zeros((row_count * col_count, weight.shape[1]), jnp.float32)
    for frame_at in range(padded.shape[0]):
        for row_at in range(3):
            for col_at in range(3):
                tap_index = (frame_at * 3 + row_at) * 3 + col_at
                window = padded[
                    frame_at, row_at : row_at + row_count, col_at : col_at + col_count
                ].reshape(row_count * col_count, channels)
                summed = summed + jnp.dot(
                    window,
                    weight[tap_index * channels : (tap_index + 1) * channels],
                    preferred_element_type=jnp.float32,
                )
    return summed


def unfold_taps(padded, row_count, col_count):
    pieces = []
    for frame_at in range(padded.shape[0]):
        for row_at in range(3):
            for col_at in range(3):
                pieces.append(
                    padded[frame_at, row_at : row_at + row_count, col_at : col_at + col_count]
                )
    joined = jnp.concatenate(pieces, axis=-1)
    return joined.reshape(row_count * col_count, joined.shape[-1])


def token_routes(first, count, breadth, slot_cap, tile_rows, tile_cols, across, shard_count):
    offset = jnp.arange(slot_cap, dtype=jnp.int32)
    position = first[..., None] + offset
    live = offset < count[..., None]
    glob_row = position // breadth
    glob_col = position % breadth
    owner = jnp.where(live, glob_row // tile_rows * across + glob_col // tile_cols, shard_count)
    place = glob_row % tile_rows * tile_cols + glob_col % tile_cols
    return (owner, place)


def per_device(
    latent_shards,
    shard_starts,
    frame_dims,
    latent_cache,
    feature_cache,
    in_weight,
    in_bias,
    norm_gain,
    res_weight,
    res_bias,
    up_weight,
    up_bias,
):
    channels = in_bias.shape[0]
    latent_width = in_weight.shape[0] // 27
    out_width = up_bias.shape[0]
    tile_rows = feature_cache.shape[2]
    tile_cols = feature_cache.shape[3] // channels
    tile_cells = tile_rows * tile_cols
    across = lax.axis_size("tx")
    down_count = lax.axis_size("ty")
    shard_count = down_count * across
    row_index = lax.axis_index("ty")
    col_index = lax.axis_index("tx")
    myself = row_index * across + col_index
    height = frame_dims[0, 0]
    breadth = frame_dims[0, 1]
    starts = shard_starts[0]
    slot_cap = latent_shards.shape[1] // latent_width
    everything = lax.all_gather(latent_shards, ("ty", "tx"), axis=1, tiled=True).reshape(
        shard_count * slot_cap, latent_width
    )
    owner, place = token_routes(
        starts[:-1],
        starts[1:] - starts[:-1],
        breadth,
        slot_cap,
        tile_rows,
        tile_cols,
        across,
        shard_count,
    )
    target = jnp.where(owner == myself, place, tile_cells).reshape(-1)
    current = (
        jnp.zeros((tile_cells, latent_width), jnp.bfloat16).at[target].set(everything, mode="drop")
    )
    ycoord = row_index * tile_rows + jnp.arange(tile_rows, dtype=jnp.int32)
    xcoord = col_index * tile_cols + jnp.arange(tile_cols, dtype=jnp.int32)
    keep = ((ycoord[:, None] < height) & (xcoord[None, :] < breadth)).astype(jnp.float32)
    keep_low = keep.astype(jnp.bfloat16)[None, :, :, None]
    keep_flat = keep.reshape(-1, 1)
    lat_stack = (
        jnp.concatenate(
            [
                latent_cache[0].reshape(2, tile_rows, tile_cols, latent_width),
                current.reshape(1, tile_rows, tile_cols, latent_width),
            ],
            0,
        )
        * keep_low
    )
    lat_padded = padded_2(lat_stack, (("ty", 1), ("tx", 2)), 1)
    unfolded = unfold_taps(lat_padded, tile_rows, tile_cols)
    first_out = (jnp.dot(unfolded, in_weight, preferred_element_type=jnp.float32) + in_bias).astype(
        jnp.bfloat16
    )
    values = first_out.astype(jnp.float32)
    power = jnp.mean(values * values, axis=1, keepdims=True)
    normed = values * lax.rsqrt(power + EPS) * norm_gain
    hidden = (jax.nn.silu(normed) * keep_flat).astype(jnp.bfloat16)
    feat_stack = jnp.concatenate(
        [
            feature_cache[0].reshape(2, tile_rows, tile_cols, channels) * keep_low,
            hidden.reshape(1, tile_rows, tile_cols, channels),
        ],
        0,
    )
    feat_padded = padded_2(feat_stack, (("ty", 1), ("tx", 2)), 1)
    branch = tap_sum(feat_padded, res_weight, tile_rows, tile_cols)
    mixed = (
        ((values + branch + res_bias) * keep_flat)
        .astype(jnp.bfloat16)
        .reshape(tile_rows, tile_cols, channels)
    )
    low_padded = padded_2(mixed, (("ty", 0), ("tx", 1)), 1)
    grown_padded = jnp.repeat(jnp.repeat(low_padded, 2, axis=0), 2, axis=1)[1:-1, 1:-1]
    result = tap_sum(grown_padded[None], up_weight, 2 * tile_rows, 2 * tile_cols) + up_bias
    keep_high = jnp.repeat(jnp.repeat(keep, 2, axis=0), 2, axis=1).reshape(-1, 1)
    return (
        (result * keep_high)
        .astype(jnp.bfloat16)
        .reshape(1, 2 * tile_rows, 2 * tile_cols * out_width)
    )


def solution(mesh):
    return jax.shard_map(
        per_device,
        mesh=mesh,
        in_specs=(
            P("vid", ("ty", "tx")),
            P("vid", None),
            P("vid", None),
            P("vid", None, "ty", "tx"),
            P("vid", None, "ty", "tx"),
            P(),
            P(),
            P(),
            P(),
            P(),
            P(),
            P(),
        ),
        out_specs=P("vid", "ty", "tx"),
        check_vma=False,
    )
```

profile of v0, /device:TPU:1, one launch (start us, length us, event | category | flops | bytes accessed | tf_op | source)
XLA Modules:
  0.0 160.1 jit_solution(8422800603614920463)
XLA Ops:
  0.7 0.8 bitcast_subtract_fusion
  1.5 1.3 fusion.105
  4.7 1.3 fusion.94
  6.2 1.0 fusion.95
  7.5 11.2 %all_gather.3 = bf16[1,99328]{1,0:T(2,128)(2,1)S(1)} all-gather(bf16[1,12416]{1,0:T(2,128)(2,1)} %param.12), channel_id=1, replica_groups=mesh['vid'=4,'ty'=2,'tx'=4] {'ty','tx'}, dimensions={1}, use_global_device_ids=true | all-gather | bytes 223488 | tf_op jit(solution)/shard_map/all_gather | solution.py:93
  18.7 1.2 reduce.1
  20.0 1.0 reshape.439
  23.1 24.5 %scatter_custom_fusion = bf16[512,16]{1,0:T(8,128)(2,1)S(1)} fusion(s32[6208]{0:T(1024)S(1)} %fusion.97, bf16[6208,16]{1,0:T(8,128)(2,1)S(1)} %reshape.439, bf16[]{:T(256)} %constant.70.clone.1), kind=kCustom, calls=%fused_computation.159 | custom fusion | bytes 16386 | tf_op jit(solution)/shard_map/scatter | solution.py:108
  47.8 2.9 %collective-permute-start = (bf16[3,1,32,16]{3,2,1,0:T(8,128)(2,1)S(1)}, bf16[3,1,32,16]{3,2,1,0:T(8,128)(2,1)S(1)}, u32[]{:S(2)}, u32[]{:S(2)}) collective-permute-start(bf16[3,1,32,16]{3,2,1,0:T(8,128)(2,1)S(1)} %get-tuple-element.84), channel_id=1, source_target_pairs={{0,4},{1,5},{2,6},{3,7},{8,12},{9,13},{10,14},{11,15},{16,20},{17,... | collective-permute-start | bytes 9224 | tf_op jit(solution)/shard_map/ppermute | solution.py:16
  50.6 1.3 collective-permute-start.1
  52.3 1.4 fusion.72
  53.7 1.5 collective-permute-done.1
  56.2 3.5 %collective-permute-start.3 = (bf16[3,18,1,16]{3,2,1,0:T(2,128)(2,1)}, bf16[3,18,1,16]{3,2,1,0:T(2,128)(2,1)}, u32[]{:S(2)}, u32[]{:S(2)}) collective-permute-start(bf16[3,18,1,16]{3,2,1,0:T(2,128)(2,1)} %get-tuple-element.68), channel_id=1, source_target_pairs={{1,0},{2,1},{3,2},{5,4},{6,5},{7,6},{9,8},{10,9},{11,10},{13,12},{... | collective-permute-start | bytes 5192 | tf_op jit(solution)/shard_map/ppermute | solution.py:17
  59.7 2.5 %collective-permute-start.2 = (bf16[3,18,1,16]{3,2,1,0:T(2,128)(2,1)}, bf16[3,18,1,16]{3,2,1,0:T(2,128)(2,1)}, u32[]{:S(2)}, u32[]{:S(2)}) collective-permute-start(bf16[3,18,1,16]{3,2,1,0:T(2,128)(2,1)} %get-tuple-element.69), channel_id=1, source_target_pairs={{0,1},{1,2},{2,3},{4,5},{5,6},{6,7},{8,9},{9,10},{10,11},{12,13},{... | collective-permute-start | bytes 5192 | tf_op jit(solution)/shard_map/ppermute | solution.py:16
  62.2 0.8 pad_maximum_fusion.11
  63.0 1.6 copy.41
  64.5 1.0 copy.42
  66.1 1.2 copy.23
  68.4 1.2 copy.19
  88.7 1.7 %multiply_reduce_fusion = (f32[512]{0:T(512)S(1)}, f32[512,384]{1,0:T(8,128)S(1)}) fusion(f32[384]{0:T(512)S(1)} %copy-done.16, bf16[512,432]{0,1:T(8,128)(2,1)} %constant_dynamic-update-slice_fusion, bf16[432,384]{1,0:T(8,128)(2,1)S(1)} %copy-done), kind=kOutput, calls=%fused_computation.50 | convolution fusion | flops 170851840 | bytes 1564160 | tf_op jit(solution)/shard_map/dot_general | solution.py:127
  90.8 2.3 %collective-permute-start.4 = (bf16[3,1,32,384]{3,2,1,0:T(8,128)(2,1)S(1)}, bf16[3,1,32,384]{3,2,1,0:T(8,128)(2,1)S(1)}, u32[]{:S(2)}, u32[]{:S(2)}) collective-permute-start(bf16[3,1,32,384]{3,2,1,0:T(8,128)(2,1)S(1)} %get-tuple-element.45), channel_id=1, source_target_pairs={{0,4},{1,5},{2,6},{3,7},{8,12},{9,13},{10,14},{11,15},{16,20},{17,... | collective-permute-start | bytes 221192 | tf_op jit(solution)/shard_map/ppermute | solution.py:16
  93.1 1.3 collective-permute-start.5
  94.4 1.4 fusion.38
  95.7 2.9 %collective-permute-done.5 = bf16[3,1,32,384]{3,2,1,0:T(8,128)(2,1)S(1)} collective-permute-done((bf16[3,1,32,384]{3,2,1,0:T(8,128)(2,1)S(1)}, bf16[3,1,32,384]{3,2,1,0:T(8,128)(2,1)S(1)}, u32[]{:S(2)}, u32[]{:S(2)}) %collective-permute-start.5) | collective-permute-done | bytes 73760 | tf_op jit(solution)/shard_map/ppermute | solution.py:17
  99.0 1.4 fusion.78
  100.5 3.3 %collective-permute-start.6 = (bf16[3,18,1,384]{3,2,1,0:T(2,128)(2,1)S(1)}, bf16[3,18,1,384]{3,2,1,0:T(2,128)(2,1)S(1)}, u32[]{:S(2)}, u32[]{:S(2)}) collective-permute-start(bf16[3,18,1,384]{3,2,1,0:T(2,128)(2,1)S(1)} %get-tuple-element.34), channel_id=1, source_target_pairs={{0,1},{1,2},{2,3},{4,5},{5,6},{6,7},{8,9},{9,10},{10,11},{12,13},{... | collective-permute-start | bytes 124424 | tf_op jit(solution)/shard_map/ppermute | solution.py:16
  103.8 2.1 %collective-permute-start.7 = (bf16[3,18,1,384]{3,2,1,0:T(2,128)(2,1)S(1)}, bf16[3,18,1,384]{3,2,1,0:T(2,128)(2,1)S(1)}, u32[]{:S(2)}, u32[]{:S(2)}) collective-permute-start(bf16[3,18,1,384]{3,2,1,0:T(2,128)(2,1)S(1)} %get-tuple-element.35), channel_id=1, source_target_pairs={{1,0},{2,1},{3,2},{5,4},{6,5},{7,6},{9,8},{10,9},{11,10},{13,12},{... | collective-permute-start | bytes 124424 | tf_op jit(solution)/shard_map/ppermute | solution.py:17
  106.0 1.4 fusion.55
  109.0 1.3 fusion.33
  110.3 1.9 %maximum_maximum_fusion = (bf16[3,18,33,384]{3,2,1,0:T(8,128)(2,1)S(1)}, bf16[3,18,33,384]{3,2,1,0:T(8,128)(2,1)S(1)}) fusion(bf16[3,1,32,384]{3,2,1,0:T(8,128)(2,1)S(1)} %collective-permute-done.5, bf16[1,16,32,384]{3,2,1,0:T(8,128)(2,1)S(1)} %bitcast.185, bf16[2,16,32,384]{3,2,1,0:T(8,128)(2,1)S(1)} %bitcast_multiply_fusion, ...), kind=kLoop, calls=%fused_computation.13 | loop fusion | flops 13685760 | bytes 4147200 | tf_op jit(solution)/shard_map/concatenate | solution.py:18
  112.2 2.0 %fusion.101 = (bf16[1,16,32,384]{3,2,1,0:T(8,128)(2,1)}, bf16[1,16,32,384]{3,2,1,0:T(8,128)(2,1)}, bf16[1,16,32,384]{3,2,1,0:T(8,128)(2,1)S(1)}, bf16[1,16,32,38...) fusion(bf16[3,18,33,384]{3,2,1,0:T(8,128)(2,1)S(1)} %get-tuple-, ...), kind=kLoop, calls=%fused_computation.218 | loop fusion | bytes 14155776 | tf_op jit(solution)/shard_map/slice | solution.py:29
  120.7 0.8 fusion.13
  121.5 0.8 fusion.21
  123.3 1.4 collective-permute-start.8
  124.8 1.3 collective-permute-start.9
  126.1 3.3 %collective-permute-done.9 = bf16[1,32,384]{2,1,0:T(8,128)(2,1)S(1)} collective-permute-done((bf16[1,32,384]{2,1,0:T(8,128)(2,1)S(1)}, bf16[1,32,384]{2,1,0:T(8,128)(2,1)S(1)}, u32[]{:S(2)}, u32[]{:S(2)}) %collective-permute-start.9) | collective-permute-done | bytes 24608 | tf_op jit(solution)/shard_map/ppermute | solution.py:17
  129.4 5.1 %collective-permute-start.10 = (bf16[18,1,384]{2,1,0:T(2,128)(2,1)S(1)}, bf16[18,1,384]{2,1,0:T(2,128)(2,1)S(1)}, u32[]{:S(2)}, u32[]{:S(2)}) collective-permute-start(bf16[18,1,384]{2,1,0:T(2,128)(2,1)S(1)} %get-tuple-element.48), channel_id=1, source_target_pairs={{0,1},{1,2},{2,3},{4,5},{5,6},{6,7},{8,9},{9,10},{10,11},{12,13},{... | collective-permute-start | bytes 41480 | tf_op jit(solution)/shard_map/ppermute | solution.py:16
  134.5 2.2 %collective-permute-start.11 = (bf16[18,1,384]{2,1,0:T(2,128)(2,1)S(1)}, bf16[18,1,384]{2,1,0:T(2,128)(2,1)S(1)}, u32[]{:S(2)}, u32[]{:S(2)}) collective-permute-start(bf16[18,1,384]{2,1,0:T(2,128)(2,1)S(1)} %get-tuple-element.49), channel_id=1, source_target_pairs={{1,0},{2,1},{3,2},{5,4},{6,5},{7,6},{9,8},{10,9},{11,10},{13,12},{... | collective-permute-start | bytes 41480 | tf_op jit(solution)/shard_map/ppermute | solution.py:17
  137.2 2.5 %collective-permute-done.11 = bf16[18,1,384]{2,1,0:T(2,128)(2,1)S(1)} collective-permute-done((bf16[18,1,384]{2,1,0:T(2,128)(2,1)S(1)}, bf16[18,1,384]{2,1,0:T(2,128)(2,1)S(1)}, u32[]{:S(2)}, u32[]{:S(2)}) %collective-permute-start.11) | collective-permute-done | bytes 13856 | tf_op jit(solution)/shard_map/ppermute | solution.py:17
  140.0 2.2 %broadcast_in_dim.42 = bf16[36,34,2,384]{3,2,1,0:T(2,128)(2,1)} broadcast(bf16[36,34,384]{2,1,0:T(8,128)(2,1)S(1)} %bitcast.197), dimensions={0,1,3} | broadcast | bytes 2820096 | tf_op jit(solution)/shard_map/broadcast_in_dim | solution.py:149
  142.2 4.2 %reshape.431 = bf16[36,68,384]{2,1,0:T(8,128)(2,1)S(1)} reshape(bf16[36,34,2,384]{3,2,1,0:T(2,128)(2,1)} %broadcast_in_dim.42) | data formatting | bytes 3760128 | tf_op jit(solution)/shard_map/reshape | solution.py:149
  146.4 0.9 slice_bitcast_fusion
  147.3 3.6 %fusion.100 = (bf16[1,32,64,384]{3,2,1,0:T(8,128)(2,1)S(1)}, bf16[1,32,64,384]{3,2,1,0:T(8,128)(2,1)S(1)}, bf16[1,32,64,384]{3,2,1,0:T(8,128)(2,1)S(1)}, bf16[1,...) fusion(bf16[1,34,66,384]{3,2,1,0:T(8,128)(2,1)S(1)} %slice_bitc, ...), kind=kLoop, calls=%fused_computation.217 | loop fusion | bytes 28311552 | tf_op jit(solution)/shard_map/slice | solution.py:29
  153.1 0.7 convolution_add_fusion.5
  153.8 0.7 convolution_add_fusion.4
  154.6 0.7 convolution_add_fusion.3
  156.0 0.7 convolution_add_fusion.1
  158.0 2.1 %reshape.433 = bf16[1,32,12288]{2,1,0:T(8,128)(2,1)} reshape(bf16[2048,192]{1,0:T(8,128)(2,1)S(1)} %copy.50) | data formatting | bytes 1572864 | tf_op jit(solution)/shard_map/reshape | solution.py:155
  (177 shorter events, 40.4 us)
Async XLA Ops:
  0.0 88.7 %copy-start = (bf16[432,384]{1,0:T(8,128)(2,1)S(1)}, bf16[432,384]{1,0:T(8,128)(2,1)}, u32[]{:S(2)}) copy-start(bf16[432,384]{1,0:T(8,128)(2,1)} %param.17) | copy-start | bytes 995332
  0.0 21.6 %copy-start.12 = (bf16[1,2,16,512]{3,2,1,0:T(8,128)(2,1)S(1)}, bf16[1,2,16,512]{3,2,1,0:T(8,128)(2,1)}, u32[]{:S(2)}) copy-start(bf16[1,2,16,512]{3,2,1,0:T(8,128)(2,1)} %param.15) | copy-start | bytes 98308
  20.0 32.0 %copy-start.9 = (bf16[1,2,16,12288]{3,2,1,0:T(8,128)(2,1)S(1)}, bf16[1,2,16,12288]{3,2,1,0:T(8,128)(2,1)}, u32[]{:S(2)}) copy-start(bf16[1,2,16,12288]{3,2,1,0:T(8,128)(2,1)} %param.16) | copy-start | bytes 2359300
  47.8 6.0 %collective-permute-start = (bf16[3,1,32,16]{3,2,1,0:T(8,128)(2,1)S(1)}, bf16[3,1,32,16]{3,2,1,0:T(8,128)(2,1)S(1)}, u32[]{:S(2)}, u32[]{:S(2)}) collective-permute-start(bf16[3,1,32,16]{3,2,1,0:T(8,128)(2,1)S(1)} %get-tuple-element.84), channel_id=1, source_target_pairs={{0,4},{1,5},{2,6},{3,7},{8,12},{9,13},{10,14},{11,15},{16,20},{17,... | collective-permute-start | bytes 9224 | tf_op jit(solution)/shard_map/ppermute | solution.py:16
  50.6 4.6 %collective-permute-start.1 = (bf16[3,1,32,16]{3,2,1,0:T(8,128)(2,1)S(1)}, bf16[3,1,32,16]{3,2,1,0:T(8,128)(2,1)S(1)}, u32[]{:S(2)}, u32[]{:S(2)}) collective-permute-start(bf16[3,1,32,16]{3,2,1,0:T(8,128)(2,1)S(1)} %get-tuple-element.85), channel_id=1, source_target_pairs={{4,0},{5,1},{6,2},{7,3},{12,8},{13,9},{14,10},{15,11},{20,16},{21,... | collective-permute-start | bytes 9224 | tf_op jit(solution)/shard_map/ppermute | solution.py:17
  56.2 9.9 %collective-permute-start.3 = (bf16[3,18,1,16]{3,2,1,0:T(2,128)(2,1)}, bf16[3,18,1,16]{3,2,1,0:T(2,128)(2,1)}, u32[]{:S(2)}, u32[]{:S(2)}) collective-permute-start(bf16[3,18,1,16]{3,2,1,0:T(2,128)(2,1)} %get-tuple-element.68), channel_id=1, source_target_pairs={{1,0},{2,1},{3,2},{5,4},{6,5},{7,6},{9,8},{10,9},{11,10},{13,12},{... | collective-permute-start | bytes 5192 | tf_op jit(solution)/shard_map/ppermute | solution.py:17
  59.7 8.7 %collective-permute-start.2 = (bf16[3,18,1,16]{3,2,1,0:T(2,128)(2,1)}, bf16[3,18,1,16]{3,2,1,0:T(2,128)(2,1)}, u32[]{:S(2)}, u32[]{:S(2)}) collective-permute-start(bf16[3,18,1,16]{3,2,1,0:T(2,128)(2,1)} %get-tuple-element.69), channel_id=1, source_target_pairs={{0,1},{1,2},{2,3},{4,5},{5,6},{6,7},{8,9},{9,10},{10,11},{12,13},{... | collective-permute-start | bytes 5192 | tf_op jit(solution)/shard_map/ppermute | solution.py:16
  70.8 2.2 %copy-start.10 = (bf16[512,16]{0,1:T(8,128)(2,1)S(1)}, bf16[512,16]{0,1:T(8,128)(2,1)}, u32[]{:S(2)}) copy-start(bf16[512,16]{0,1:T(8,128)(2,1)} %copy.41) | copy-start | bytes 49156
  70.8 2.8 %copy-start.11 = (bf16[512,16]{0,1:T(8,128)(2,1)S(1)}, bf16[512,16]{0,1:T(8,128)(2,1)}, u32[]{:S(2)}) copy-start(bf16[512,16]{0,1:T(8,128)(2,1)} %concatenate.149) | copy-start | bytes 49156
  71.3 17.4 %copy-start.16 = (f32[384]{0:T(512)S(1)}, f32[384]{0:T(512)}, u32[]{:S(2)}) copy-start(f32[384]{0:T(512)} %param.18) | copy-start | bytes 4612
  72.6 17.8 %copy-start.13 = (f32[384]{0:T(512)S(1)}, f32[384]{0:T(512)}, u32[]{:S(2)}) copy-start(f32[384]{0:T(512)} %param.19) | copy-start | bytes 4612
  88.7 18.6 %slice-start = ((s8[7962624]{0:T(1024)(128)(4,1)}), s8[4194304]{0:T(1024)(128)(4,1)S(1)}, s32[]{:S(2)}) async-start(s8[7962624]{0:T(1024)(128)(4,1)} %bitcast.186), calls=%async_computation | async-start | bytes 8388608
  90.8 4.9 %collective-permute-start.4 = (bf16[3,1,32,384]{3,2,1,0:T(8,128)(2,1)S(1)}, bf16[3,1,32,384]{3,2,1,0:T(8,128)(2,1)S(1)}, u32[]{:S(2)}, u32[]{:S(2)}) collective-permute-start(bf16[3,1,32,384]{3,2,1,0:T(8,128)(2,1)S(1)} %get-tuple-element.45), channel_id=1, source_target_pairs={{0,4},{1,5},{2,6},{3,7},{8,12},{9,13},{10,14},{11,15},{16,20},{17,... | collective-permute-start | bytes 221192 | tf_op jit(solution)/shard_map/ppermute | solution.py:16
  93.1 5.6 %collective-permute-start.5 = (bf16[3,1,32,384]{3,2,1,0:T(8,128)(2,1)S(1)}, bf16[3,1,32,384]{3,2,1,0:T(8,128)(2,1)S(1)}, u32[]{:S(2)}, u32[]{:S(2)}) collective-permute-start(bf16[3,1,32,384]{3,2,1,0:T(8,128)(2,1)S(1)} %get-tuple-element.46), channel_id=1, source_target_pairs={{4,0},{5,1},{6,2},{7,3},{12,8},{13,9},{14,10},{15,11},{20,16},{21,... | collective-permute-start | bytes 221192 | tf_op jit(solution)/shard_map/ppermute | solution.py:17
  95.7 11.6 %slice-start.1 = ((s8[7962624]{0:T(1024)(128)(4,1)}), s8[3768320]{0:T(1024)(128)(4,1)S(1)}, s32[]{:S(2)}) async-start(s8[7962624]{0:T(1024)(128)(4,1)} %bitcast.186), calls=%async_computation.1 | async-start | bytes 7536640
  100.5 9.7 %collective-permute-start.6 = (bf16[3,18,1,384]{3,2,1,0:T(2,128)(2,1)S(1)}, bf16[3,18,1,384]{3,2,1,0:T(2,128)(2,1)S(1)}, u32[]{:S(2)}, u32[]{:S(2)}) collective-permute-start(bf16[3,18,1,384]{3,2,1,0:T(2,128)(2,1)S(1)} %get-tuple-element.34), channel_id=1, source_target_pairs={{0,1},{1,2},{2,3},{4,5},{5,6},{6,7},{8,9},{9,10},{10,11},{12,13},{... | collective-permute-start | bytes 124424 | tf_op jit(solution)/shard_map/ppermute | solution.py:16
  103.8 6.4 %collective-permute-start.7 = (bf16[3,18,1,384]{3,2,1,0:T(2,128)(2,1)S(1)}, bf16[3,18,1,384]{3,2,1,0:T(2,128)(2,1)S(1)}, u32[]{:S(2)}, u32[]{:S(2)}) collective-permute-start(bf16[3,18,1,384]{3,2,1,0:T(2,128)(2,1)S(1)} %get-tuple-element.35), channel_id=1, source_target_pairs={{1,0},{2,1},{3,2},{5,4},{6,5},{7,6},{9,8},{10,9},{11,10},{13,12},{... | collective-permute-start | bytes 124424 | tf_op jit(solution)/shard_map/ppermute | solution.py:17
  117.8 1.0 copy-start.7
  118.2 1.0 copy-start.6
  118.6 1.1 copy-start.5
  119.2 1.0 copy-start.4
  121.5 1.1 copy-start.2
  121.5 1.2 copy-start.3
  121.5 1.2 copy-start.14
  123.3 2.7 %collective-permute-start.8 = (bf16[1,32,384]{2,1,0:T(8,128)(2,1)S(1)}, bf16[1,32,384]{2,1,0:T(8,128)(2,1)S(1)}, u32[]{:S(2)}, u32[]{:S(2)}) collective-permute-start(bf16[1,32,384]{2,1,0:T(8,128)(2,1)S(1)} %get-tuple-element.76), channel_id=1, source_target_pairs={{0,4},{1,5},{2,6},{3,7},{8,12},{9,13},{10,14},{11,15},{16,20},{17,... | collective-permute-start | bytes 73736 | tf_op jit(solution)/shard_map/ppermute | solution.py:16
  124.8 4.6 %collective-permute-start.9 = (bf16[1,32,384]{2,1,0:T(8,128)(2,1)S(1)}, bf16[1,32,384]{2,1,0:T(8,128)(2,1)S(1)}, u32[]{:S(2)}, u32[]{:S(2)}) collective-permute-start(bf16[1,32,384]{2,1,0:T(8,128)(2,1)S(1)} %get-tuple-element.77), channel_id=1, source_target_pairs={{4,0},{5,1},{6,2},{7,3},{12,8},{13,9},{14,10},{15,11},{20,16},{21,... | collective-permute-start | bytes 73736 | tf_op jit(solution)/shard_map/ppermute | solution.py:17
  129.4 7.8 %collective-permute-start.10 = (bf16[18,1,384]{2,1,0:T(2,128)(2,1)S(1)}, bf16[18,1,384]{2,1,0:T(2,128)(2,1)S(1)}, u32[]{:S(2)}, u32[]{:S(2)}) collective-permute-start(bf16[18,1,384]{2,1,0:T(2,128)(2,1)S(1)} %get-tuple-element.48), channel_id=1, source_target_pairs={{0,1},{1,2},{2,3},{4,5},{5,6},{6,7},{8,9},{9,10},{10,11},{12,13},{... | collective-permute-start | bytes 41480 | tf_op jit(solution)/shard_map/ppermute | solution.py:16
  134.5 5.2 %collective-permute-start.11 = (bf16[18,1,384]{2,1,0:T(2,128)(2,1)S(1)}, bf16[18,1,384]{2,1,0:T(2,128)(2,1)S(1)}, u32[]{:S(2)}, u32[]{:S(2)}) collective-permute-start(bf16[18,1,384]{2,1,0:T(2,128)(2,1)S(1)} %get-tuple-element.49), channel_id=1, source_target_pairs={{1,0},{2,1},{3,2},{5,4},{6,5},{7,6},{9,8},{10,9},{11,10},{13,12},{... | collective-permute-start | bytes 41480 | tf_op jit(solution)/shard_map/ppermute | solution.py:17
  147.3 3.6 %copy-start.8 = (bf16[3456,192]{0,1:T(8,128)(2,1)S(1)}, bf16[3456,192]{0,1:T(8,128)(2,1)}, u32[]{:S(2)}) copy-start(bf16[3456,192]{0,1:T(8,128)(2,1)} %param.22) | copy-start | bytes 3981316
  156.0 0.7 copy-start.15
  156.8 3.3 %copy-start.1 = (bf16[432,384]{1,0:T(8,128)(2,1)S(1)}, bf16[432,384]{1,0:T(8,128)(2,1)}, u32[]{:S(2)}) copy-start(bf16[432,384]{1,0:T(8,128)(2,1)} %param.17) | copy-start | bytes 995332
where the time goes:
time: 161 us; the launch traced here: 160 us
  local copies, waits for them, and re-layouts  71.1 us (44%)
  starting transfers between devices  29.1 us (18%)
  matrix products  24.5 us (15%)
  blocking collectives  11.2 us (7%)
  other arithmetic  11.1 us (7%)
  waiting for transfers between devices  10.2 us (6%)
  between operations  2.86 us (2%)
    scatter x1, local copies, waits for them, and re-layouts, per_device(): jnp.zeros((tile_cells, latent_width), jnp.bfloat16).at[target]  24.5 us
    dot_general x36, matrix products, tap_sum(): jnp.dot(window, weight[tap_index * channels:(tap_index + 1) * channels],...  22.8 us
    ppermute x6, starting transfers between devices, padded_2(): before = lax.ppermute(last, axis, up)  17.4 us
    unnamed x65, local copies, waits for them, and re-layouts  16.8 us
    ppermute x6, starting transfers between devices, padded_2(): after = lax.ppermute(leading, axis, down)  11.7 us
    all_gather x1, blocking collectives, per_device(): lax.all_gather(latent_shards, ('ty', 'tx'), axis=1, tiled=True)  11.2 us
    ppermute x6, waiting for transfers between devices, padded_2(): after = lax.ppermute(leading, axis, down)  10.2 us
    concatenate x28, local copies, waits for them, and re-layouts, unfold_taps(): joined = jnp.concatenate(pieces, axis=-1)  6.48 us
  transfers between devices with their start and end apart: 12, of which 4 were waited for; matrix products, arithmetic and copies ran while one was open for 9% of the time, Pallas kernels for 0%

commit v1 on v0

--- a/solution.py
+++ b/solution.py
@@ -4,6 +4,32 @@
 from jax.sharding import PartitionSpec as P
 
 EPS = 1e-06
+
+
+def _play_blocks(vals, on_dim):
+    carry_in = list(vals.shape[1:])
+    carry_in[on_dim] *= vals.shape[0]
+    return jnp.moveaxis(vals, 0, on_dim).reshape(carry_in)
+
+
+def table_detail(pos_dim, unit, lane_axis):
+    q_n = lax.axis_size(lane_axis)
+    copies = tuple(((p, (p + 1) % q_n) for p in range(q_n)))
+    block_list = tuple(((j0, ix) for ix, j0 in copies))
+    mixed_arr, m_next = ([], [])
+    for rr in range(q_n - 1):
+        if rr % 2 == 0:
+            all_values = lax.ppermute(mixed_arr[-1] if mixed_arr else unit, lane_axis, copies)
+            mixed_arr.append(all_values)
+        else:
+            side_arr = lax.ppermute(m_next[-1] if m_next else unit, lane_axis, block_list)
+            m_next.append(side_arr)
+    block_now = jnp.stack([*mixed_arr[::-1], unit, *m_next], 0)
+    tmp = lax.axis_index(lane_axis)
+    arr_now = len(mixed_arr)
+    current_block = tmp - arr_now
+    block_now = block_now[(jnp.arange(q_n) - current_block) % q_n]
+    return _play_blocks(block_now, pos_dim)
 
 
 def padded_2(value, sides, width):
@@ -90,7 +116,7 @@
     breadth = frame_dims[0, 1]
     starts = shard_starts[0]
     slot_cap = latent_shards.shape[1] // latent_width
-    everything = lax.all_gather(latent_shards, ("ty", "tx"), axis=1, tiled=True).reshape(
+    everything = table_detail(1, latent_shards, ("ty", "tx")).reshape(
         shard_count * slot_cap, latent_width
     )
     owner, place = token_routes(

time: 161 us -> 172 us (1.068)
  blocking collectives: 11.2 us -> 0 us
  starting transfers between devices: 29.1 us -> 40.2 us
  local copies, waits for them, and re-layouts: 71.1 us -> 79.1 us
  waiting for transfers between devices: 10.2 us -> 13.5 us
    all_gather x1 -> x0, blocking collectives: 11.2 us -> none  [per_device(): lax.all_gather(latent_shards, ('ty', 'tx'), axis=1, tiled=True)]
    ppermute x0 -> x7, starting transfers between devices: none -> 9.13 us  [the longest x4 9.07 us: table_detail(): lax.ppermute(mixed_arr[-1] if mixed_arr else unit, lane_axis, copies)]
    ppermute x6, starting transfers between devices: 11.7 us -> 16.8 us  [padded_2(): after = lax.ppermute(leading, axis, down)]
    another operation x0 -> x2, local copies, waits for them, and re-layouts: none -> 3.8 us  [the longest x1 2.09 us: per_device(): table_detail(1, latent_shards, ('ty', 'tx'))]
    ppermute x6, starting transfers between devices: 17.4 us -> 14.2 us  [padded_2(): before = lax.ppermute(last, axis, up)]
    ppermute x0 -> x7, waiting for transfers between devices: none -> 3.07 us  [the longest x4 1.87 us: table_detail(): lax.ppermute(mixed_arr[-1] if mixed_arr else unit, lane_axis, copies)]
    concatenate x28, local copies, waits for them, and re-layouts: 6.48 us -> 8.59 us  [unfold_taps(): joined = jnp.concatenate(pieces, axis=-1)]
    unnamed x65 -> x77, local copies, waits for them, and re-layouts: 16.8 us -> 18.4 us
  transfers between devices with their start and end apart: 12 -> 19, of which waited for: 4 -> 9; matrix products, arithmetic and copies ran while one was open for 9% -> 15% of each run, Pallas kernels for 0% -> 0%
where the time goes in v1:
time: 172 us; the launch traced here: 171 us
  local copies, waits for them, and re-layouts  79.1 us (46%)
  starting transfers between devices  40.2 us (23%)
  matrix products  24.5 us (14%)
  waiting for transfers between devices  13.5 us (8%)
  other arithmetic  10.6 us (6%)
  between operations  2.88 us (2%)
    scatter x1, local copies, waits for them, and re-layouts, per_device(): jnp.zeros((tile_cells, latent_width), jnp.bfloat16).at[target]  24.5 us
    dot_general x36, matrix products, tap_sum(): jnp.dot(window, weight[tap_index * channels:(tap_index + 1) * channels],...  22.8 us
    unnamed x77, local copies, waits for them, and re-layouts  18.4 us
    ppermute x6, starting transfers between devices, padded_2(): after = lax.ppermute(leading, axis, down)  16.8 us
    ppermute x6, starting transfers between devices, padded_2(): before = lax.ppermute(last, axis, up)  14.2 us
    ppermute x6, waiting for transfers between devices, padded_2(): after = lax.ppermute(leading, axis, down)  10.4 us
    ppermute x4, starting transfers between devices, table_detail(): lax.ppermute(mixed_arr[-1] if mixed_arr else unit, lane_axis, copies)  9.07 us
    concatenate x28, local copies, waits for them, and re-layouts, unfold_taps(): joined = jnp.concatenate(pieces, axis=-1)  8.59 us
  transfers between devices with their start and end apart: 19, of which 9 were waited for; matrix products, arithmetic and copies ran while one was open for 15% of the time, Pallas kernels for 0%

profile of v1, /device:TPU:1, one launch (start us, length us, event | category | flops | bytes accessed | tf_op | source)
XLA Modules:
  0.0 170.8 jit_solution(2395818327588983249)
XLA Ops:
  0.0 2.6 %collective-permute-start = (bf16[1,12416]{1,0:T(2,128)(2,1)}, bf16[1,12416]{1,0:T(2,128)(2,1)S(1)}, u32[]{:S(2)}, u32[]{:S(2)}) collective-permute-start(bf16[1,12416]{1,0:T(2,128)(2,1)} %param.12), channel_id=1, source_target_pairs={{0,1},{1,2},{2,3},{3,4},{4,5},{5,6},{6,7},{7,0},{8,9},{9,10},{10,1... | collective-permute-start | bytes 74504 | tf_op jit(solution)/shard_map/ppermute | solution.py:22
  3.3 0.8 bitcast_subtract_fusion
  4.1 1.3 fusion.107
  7.2 1.2 fusion.94
  8.5 1.0 fusion.95
  10.1 1.2 copy.51
  12.8 1.8 %collective-permute-start.1 = (bf16[1,12416]{1,0:T(2,128)(2,1)S(1)}, bf16[1,12416]{1,0:T(2,128)(2,1)S(1)}, u32[]{:S(2)}, u32[]{:S(2)}) collective-permute-start(bf16[1,12416]{1,0:T(2,128)(2,1)S(1)} %collective-permute-done), channel_id=1, source_target_pairs={{0,1},{1,2},{2,3},{3,4},{4,5},{5,6},{6,7},{7,0},{8,9},{9,10},{10,1... | collective-permute-start | bytes 74504 | tf_op jit(solution)/shard_map/ppermute | solution.py:22
  15.8 2.3 %collective-permute-start.2 = (bf16[1,12416]{1,0:T(2,128)(2,1)S(1)}, bf16[1,12416]{1,0:T(2,128)(2,1)S(1)}, u32[]{:S(2)}, u32[]{:S(2)}) collective-permute-start(bf16[1,12416]{1,0:T(2,128)(2,1)S(1)} %collective-permute-done.1), channel_id=1, source_target_pairs={{0,1},{1,2},{2,3},{3,4},{4,5},{5,6},{6,7},{7,0},{8,9},{9,10},{10,1... | collective-permute-start | bytes 74504 | tf_op jit(solution)/shard_map/ppermute | solution.py:22
  19.3 2.3 %collective-permute-start.3 = (bf16[1,12416]{1,0:T(2,128)(2,1)S(1)}, bf16[1,12416]{1,0:T(2,128)(2,1)S(1)}, u32[]{:S(2)}, u32[]{:S(2)}) collective-permute-start(bf16[1,12416]{1,0:T(2,128)(2,1)S(1)} %collective-permute-done.2), channel_id=1, source_target_pairs={{0,1},{1,2},{2,3},{3,4},{4,5},{5,6},{6,7},{7,0},{8,9},{9,10},{10,1... | collective-permute-start | bytes 74504 | tf_op jit(solution)/shard_map/ppermute | solution.py:22
  23.3 1.7 %stack.35 = bf16[8,1,12416]{2,0,1:T(8,128)(2,1)S(1)} concatenate(bf16[1,1,12416]{2,0,1:T(2,128)(2,1)S(1)} %bitcast.258, bf16[1,1,12416]{2,0,1:T(2,128)(2,1)S(1)} %bitcast.256, bf16[1,1,12416]{2,0,1:T(2,128)(2,1)S(1)} %bitcast.254, bf16[1,1,12416]{2,0,1:T(2,128)(2,1)S(1)} %bitcast.252, bf16[1,1,12416]{2,0,1:T(2,128)(2,1)S(1)} %bitcast.251, bf16[1,1,12416]{2,0,1:T(2,128)(2,1)S(1)} %bitcast.253, ...), dimensions={0} | concatenate | bytes 397312 | tf_op jit(solution)/shard_map/stack | solution.py:27
  25.0 1.4 gather_fusion
  26.4 2.1 %reshape.494 = bf16[6208,16]{1,0:T(8,128)(2,1)S(1)} reshape(bf16[8,12416]{1,0:T(8,128)(2,1)} %gather_fusion) | data formatting | bytes 397312 | tf_op jit(solution)/shard_map/reshape;reshape;transpose | solution.py:119
  28.5 24.5 %scatter_custom_fusion = bf16[512,16]{1,0:T(8,128)(2,1)S(1)} fusion(s32[6208]{0:T(1024)S(1)} %fusion.97, bf16[6208,16]{1,0:T(8,128)(2,1)S(1)} %reshape.494, bf16[]{:T(256)} %constant.84.clone.1), kind=kCustom, calls=%fused_computation.160 | custom fusion | bytes 16386 | tf_op jit(solution)/shard_map/scatter | solution.py:134
  53.1 4.0 %collective-permute-start.7 = (bf16[3,1,32,16]{3,2,1,0:T(8,128)(2,1)S(1)}, bf16[3,1,32,16]{3,2,1,0:T(8,128)(2,1)S(1)}, u32[]{:S(2)}, u32[]{:S(2)}) collective-permute-start(bf16[3,1,32,16]{3,2,1,0:T(8,128)(2,1)S(1)} %get-tuple-element.84), channel_id=1, source_target_pairs={{0,4},{1,5},{2,6},{3,7},{8,12},{9,13},{10,14},{11,15},{16,20},{17,... | collective-permute-start | bytes 9224 | tf_op jit(solution)/shard_map/ppermute | solution.py:42
  57.2 1.3 collective-permute-start.8
  58.5 1.4 fusion.72
  59.9 1.8 %collective-permute-done.8 = bf16[3,1,32,16]{3,2,1,0:T(8,128)(2,1)S(1)} collective-permute-done((bf16[3,1,32,16]{3,2,1,0:T(8,128)(2,1)S(1)}, bf16[3,1,32,16]{3,2,1,0:T(8,128)(2,1)S(1)}, u32[]{:S(2)}, u32[]{:S(2)}) %collective-permute-start.8) | collective-permute-done | bytes 3104 | tf_op jit(solution)/shard_map/ppermute | solution.py:43
  62.5 7.0 %collective-permute-start.10 = (bf16[3,18,1,16]{3,2,1,0:T(2,128)(2,1)}, bf16[3,18,1,16]{3,2,1,0:T(2,128)(2,1)}, u32[]{:S(2)}, u32[]{:S(2)}) collective-permute-start(bf16[3,18,1,16]{3,2,1,0:T(2,128)(2,1)} %get-tuple-element.68), channel_id=1, source_target_pairs={{1,0},{2,1},{3,2},{5,4},{6,5},{7,6},{9,8},{10,9},{11,10},{13,12},{... | collective-permute-start | bytes 5192 | tf_op jit(solution)/shard_map/ppermute | solution.py:43
  69.5 1.5 pad_maximum_fusion.11
  71.3 1.6 copy.41
  72.9 2.1 %collective-permute-start.9 = (bf16[3,18,1,16]{3,2,1,0:T(2,128)(2,1)}, bf16[3,18,1,16]{3,2,1,0:T(2,128)(2,1)}, u32[]{:S(2)}, u32[]{:S(2)}) collective-permute-start(bf16[3,18,1,16]{3,2,1,0:T(2,128)(2,1)} %get-tuple-element.69), channel_id=1, source_target_pairs={{0,1},{1,2},{2,3},{4,5},{5,6},{6,7},{8,9},{9,10},{10,11},{12,13},{... | collective-permute-start | bytes 5192 | tf_op jit(solution)/shard_map/ppermute | solution.py:42
  75.0 1.6 copy.42
  76.6 1.6 copy.43
  78.7 1.2 copy.23
  81.0 1.2 copy.19
  101.3 1.7 %multiply_reduce_fusion = (f32[512]{0:T(512)S(1)}, f32[512,384]{1,0:T(8,128)S(1)}) fusion(f32[384]{0:T(512)S(1)} %copy-done.22, bf16[512,432]{0,1:T(8,128)(2,1)} %constant_dynamic-update-slice_fusion, bf16[432,384]{1,0:T(8,128)(2,1)S(1)} %copy-done), kind=kOutput, calls=%fused_computation.51 | convolution fusion | flops 170851840 | bytes 1564160 | tf_op jit(solution)/shard_map/dot_general | solution.py:153
  103.4 1.3 collective-permute-start.11
  104.7 1.3 collective-permute-start.12
  106.0 1.4 fusion.38
  107.4 2.4 %collective-permute-done.12 = bf16[3,1,32,384]{3,2,1,0:T(8,128)(2,1)S(1)} collective-permute-done((bf16[3,1,32,384]{3,2,1,0:T(8,128)(2,1)S(1)}, bf16[3,1,32,384]{3,2,1,0:T(8,128)(2,1)S(1)}, u32[]{:S(2)}, u32[]{:S(2)}) %collective-permute-start.12) | collective-permute-done | bytes 73760 | tf_op jit(solution)/shard_map/ppermute | solution.py:43
  110.2 1.4 fusion.78
  111.7 2.0 %collective-permute-start.13 = (bf16[3,18,1,384]{3,2,1,0:T(2,128)(2,1)S(1)}, bf16[3,18,1,384]{3,2,1,0:T(2,128)(2,1)S(1)}, u32[]{:S(2)}, u32[]{:S(2)}) collective-permute-start(bf16[3,18,1,384]{3,2,1,0:T(2,128)(2,1)S(1)} %get-tuple-element.34), channel_id=1, source_target_pairs={{0,1},{1,2},{2,3},{4,5},{5,6},{6,7},{8,9},{9,10},{10,11},{12,13},{... | collective-permute-start | bytes 124424 | tf_op jit(solution)/shard_map/ppermute | solution.py:42
  113.7 3.8 %collective-permute-start.14 = (bf16[3,18,1,384]{3,2,1,0:T(2,128)(2,1)S(1)}, bf16[3,18,1,384]{3,2,1,0:T(2,128)(2,1)S(1)}, u32[]{:S(2)}, u32[]{:S(2)}) collective-permute-start(bf16[3,18,1,384]{3,2,1,0:T(2,128)(2,1)S(1)} %get-tuple-element.35), channel_id=1, source_target_pairs={{1,0},{2,1},{3,2},{5,4},{6,5},{7,6},{9,8},{10,9},{11,10},{13,12},{... | collective-permute-start | bytes 124424 | tf_op jit(solution)/shard_map/ppermute | solution.py:43
  117.5 1.4 fusion.55
  120.5 1.3 fusion.33
  121.7 1.9 %maximum_maximum_fusion = (bf16[3,18,33,384]{3,2,1,0:T(8,128)(2,1)S(1)}, bf16[3,18,33,384]{3,2,1,0:T(8,128)(2,1)S(1)}) fusion(bf16[3,1,32,384]{3,2,1,0:T(8,128)(2,1)S(1)} %collective-permute-done.12, bf16[1,16,32,384]{3,2,1,0:T(8,128)(2,1)S(1)} %bitcast.197, bf16[2,16,32,384]{3,2,1,0:T(8,128)(2,1)S(1)} %bitcast_multiply_fusion, ...), kind=kLoop, calls=%fused_computation.14 | loop fusion | flops 13685760 | bytes 4147200 | tf_op jit(solution)/shard_map/concatenate | solution.py:44
  123.7 2.1 %fusion.103 = (bf16[1,16,32,384]{3,2,1,0:T(8,128)(2,1)}, bf16[1,16,32,384]{3,2,1,0:T(8,128)(2,1)}, bf16[1,16,32,384]{3,2,1,0:T(8,128)(2,1)S(1)}, bf16[1,16,32,38...) fusion(bf16[3,18,33,384]{3,2,1,0:T(8,128)(2,1)S(1)} %get-tuple-, ...), kind=kLoop, calls=%fused_computation.226 | loop fusion | bytes 14155776 | tf_op jit(solution)/shard_map/slice | solution.py:55
  135.4 1.4 collective-permute-start.15
  136.8 1.3 collective-permute-start.16
  138.1 3.7 %collective-permute-done.16 = bf16[1,32,384]{2,1,0:T(8,128)(2,1)S(1)} collective-permute-done((bf16[1,32,384]{2,1,0:T(8,128)(2,1)S(1)}, bf16[1,32,384]{2,1,0:T(8,128)(2,1)S(1)}, u32[]{:S(2)}, u32[]{:S(2)}) %collective-permute-start.16) | collective-permute-done | bytes 24608 | tf_op jit(solution)/shard_map/ppermute | solution.py:43
  141.9 3.3 %collective-permute-start.17 = (bf16[18,1,384]{2,1,0:T(2,128)(2,1)S(1)}, bf16[18,1,384]{2,1,0:T(2,128)(2,1)S(1)}, u32[]{:S(2)}, u32[]{:S(2)}) collective-permute-start(bf16[18,1,384]{2,1,0:T(2,128)(2,1)S(1)} %get-tuple-element.48), channel_id=1, source_target_pairs={{0,1},{1,2},{2,3},{4,5},{5,6},{6,7},{8,9},{9,10},{10,11},{12,13},{... | collective-permute-start | bytes 41480 | tf_op jit(solution)/shard_map/ppermute | solution.py:42
  145.2 2.2 %collective-permute-start.18 = (bf16[18,1,384]{2,1,0:T(2,128)(2,1)S(1)}, bf16[18,1,384]{2,1,0:T(2,128)(2,1)S(1)}, u32[]{:S(2)}, u32[]{:S(2)}) collective-permute-start(bf16[18,1,384]{2,1,0:T(2,128)(2,1)S(1)} %get-tuple-element.49), channel_id=1, source_target_pairs={{1,0},{2,1},{3,2},{5,4},{6,5},{7,6},{9,8},{10,9},{11,10},{13,12},{... | collective-permute-start | bytes 41480 | tf_op jit(solution)/shard_map/ppermute | solution.py:43
  147.9 2.5 %collective-permute-done.18 = bf16[18,1,384]{2,1,0:T(2,128)(2,1)S(1)} collective-permute-done((bf16[18,1,384]{2,1,0:T(2,128)(2,1)S(1)}, bf16[18,1,384]{2,1,0:T(2,128)(2,1)S(1)}, u32[]{:S(2)}, u32[]{:S(2)}) %collective-permute-start.18) | collective-permute-done | bytes 13856 | tf_op jit(solution)/shard_map/ppermute | solution.py:43
  150.7 2.3 %broadcast_in_dim.43 = bf16[36,34,2,384]{3,2,1,0:T(2,128)(2,1)} broadcast(bf16[36,34,384]{2,1,0:T(8,128)(2,1)S(1)} %bitcast.209), dimensions={0,1,3} | broadcast | bytes 2820096 | tf_op jit(solution)/shard_map/broadcast_in_dim | solution.py:175
  153.0 4.2 %reshape.476 = bf16[36,68,384]{2,1,0:T(8,128)(2,1)S(1)} reshape(bf16[36,34,2,384]{3,2,1,0:T(2,128)(2,1)} %broadcast_in_dim.43) | data formatting | bytes 3760128 | tf_op jit(solution)/shard_map/reshape | solution.py:175
  157.2 0.9 slice_bitcast_fusion
  158.1 3.6 %fusion.102 = (bf16[1,32,64,384]{3,2,1,0:T(8,128)(2,1)S(1)}, bf16[1,32,64,384]{3,2,1,0:T(8,128)(2,1)S(1)}, bf16[1,32,64,384]{3,2,1,0:T(8,128)(2,1)S(1)}, bf16[1,...) fusion(bf16[1,34,66,384]{3,2,1,0:T(8,128)(2,1)S(1)} %slice_bitc, ...), kind=kLoop, calls=%fused_computation.225 | loop fusion | bytes 28311552 | tf_op jit(solution)/shard_map/slice | solution.py:55
  168.8 2.1 %reshape.478 = bf16[1,32,12288]{2,1,0:T(8,128)(2,1)} reshape(bf16[2048,192]{1,0:T(8,128)(2,1)S(1)} %copy.50) | data formatting | bytes 1572864 | tf_op jit(solution)/shard_map/reshape | solution.py:181
  (205 shorter events, 48.2 us)
Async XLA Ops:
  0.0 101.3 %copy-start = (bf16[432,384]{1,0:T(8,128)(2,1)S(1)}, bf16[432,384]{1,0:T(8,128)(2,1)}, u32[]{:S(2)}) copy-start(bf16[432,384]{1,0:T(8,128)(2,1)} %param.17) | copy-start | bytes 995332
  0.0 12.8 %collective-permute-start = (bf16[1,12416]{1,0:T(2,128)(2,1)}, bf16[1,12416]{1,0:T(2,128)(2,1)S(1)}, u32[]{:S(2)}, u32[]{:S(2)}) collective-permute-start(bf16[1,12416]{1,0:T(2,128)(2,1)} %param.12), channel_id=1, source_target_pairs={{0,1},{1,2},{2,3},{3,4},{4,5},{5,6},{6,7},{7,0},{8,9},{9,10},{10,1... | collective-permute-start | bytes 74504 | tf_op jit(solution)/shard_map/ppermute | solution.py:22
  2.6 12.6 %collective-permute-start.4 = (bf16[1,12416]{1,0:T(2,128)(2,1)}, bf16[1,12416]{1,0:T(2,128)(2,1)S(1)}, u32[]{:S(2)}, u32[]{:S(2)}) collective-permute-start(bf16[1,12416]{1,0:T(2,128)(2,1)} %param.12), channel_id=1, source_target_pairs={{1,0},{2,1},{3,2},{4,3},{5,4},{6,5},{7,6},{0,7},{9,8},{10,9},{11,1... | collective-permute-start | bytes 74504 | tf_op jit(solution)/shard_map/ppermute | solution.py:25
  10.1 11.6 %copy-start.18 = (bf16[1,2,16,512]{3,2,1,0:T(8,128)(2,1)S(1)}, bf16[1,2,16,512]{3,2,1,0:T(8,128)(2,1)}, u32[]{:S(2)}) copy-start(bf16[1,2,16,512]{3,2,1,0:T(8,128)(2,1)} %param.15) | copy-start | bytes 98308
  11.4 12.0 %copy-start.17 = (bf16[1,12416]{1,0:T(2,128)(2,1)S(1)}, bf16[1,12416]{1,0:T(2,128)(2,1)}, u32[]{:S(2)}) copy-start(bf16[1,12416]{1,0:T(2,128)(2,1)} %param.12) | copy-start | bytes 74500
  12.1 47.7 %copy-start.11 = (f32[16,32]{1,0:T(8,128)}, f32[16,32]{1,0:T(8,128)S(1)}, u32[]{:S(2)}) copy-start(f32[16,32]{1,0:T(8,128)S(1)} %get-tuple-element.86) | copy-start | bytes 6148
  12.8 3.0 %collective-permute-start.1 = (bf16[1,12416]{1,0:T(2,128)(2,1)S(1)}, bf16[1,12416]{1,0:T(2,128)(2,1)S(1)}, u32[]{:S(2)}, u32[]{:S(2)}) collective-permute-start(bf16[1,12416]{1,0:T(2,128)(2,1)S(1)} %collective-permute-done), channel_id=1, source_target_pairs={{0,1},{1,2},{2,3},{3,4},{4,5},{5,6},{6,7},{7,0},{8,9},{9,10},{10,1... | collective-permute-start | bytes 74504 | tf_op jit(solution)/shard_map/ppermute | solution.py:22
  15.2 3.6 %collective-permute-start.5 = (bf16[1,12416]{1,0:T(2,128)(2,1)S(1)}, bf16[1,12416]{1,0:T(2,128)(2,1)S(1)}, u32[]{:S(2)}, u32[]{:S(2)}) collective-permute-start(bf16[1,12416]{1,0:T(2,128)(2,1)S(1)} %collective-permute-done.4), channel_id=1, source_target_pairs={{1,0},{2,1},{3,2},{4,3},{5,4},{6,5},{7,6},{0,7},{9,8},{10,9},{11,1... | collective-permute-start | bytes 74504 | tf_op jit(solution)/shard_map/ppermute | solution.py:25
  15.8 3.5 %collective-permute-start.2 = (bf16[1,12416]{1,0:T(2,128)(2,1)S(1)}, bf16[1,12416]{1,0:T(2,128)(2,1)S(1)}, u32[]{:S(2)}, u32[]{:S(2)}) collective-permute-start(bf16[1,12416]{1,0:T(2,128)(2,1)S(1)} %collective-permute-done.1), channel_id=1, source_target_pairs={{0,1},{1,2},{2,3},{3,4},{4,5},{5,6},{6,7},{7,0},{8,9},{9,10},{10,1... | collective-permute-start | bytes 74504 | tf_op jit(solution)/shard_map/ppermute | solution.py:22
  18.8 3.8 %collective-permute-start.6 = (bf16[1,12416]{1,0:T(2,128)(2,1)S(1)}, bf16[1,12416]{1,0:T(2,128)(2,1)S(1)}, u32[]{:S(2)}, u32[]{:S(2)}) collective-permute-start(bf16[1,12416]{1,0:T(2,128)(2,1)S(1)} %collective-permute-done.5), channel_id=1, source_target_pairs={{1,0},{2,1},{3,2},{4,3},{5,4},{6,5},{7,6},{0,7},{9,8},{10,9},{11,1... | collective-permute-start | bytes 74504 | tf_op jit(solution)/shard_map/ppermute | solution.py:25
  19.3 4.0 %collective-permute-start.3 = (bf16[1,12416]{1,0:T(2,128)(2,1)S(1)}, bf16[1,12416]{1,0:T(2,128)(2,1)S(1)}, u32[]{:S(2)}, u32[]{:S(2)}) collective-permute-start(bf16[1,12416]{1,0:T(2,128)(2,1)S(1)} %collective-permute-done.2), channel_id=1, source_target_pairs={{0,1},{1,2},{2,3},{3,4},{4,5},{5,6},{6,7},{7,0},{8,9},{9,10},{10,1... | collective-permute-start | bytes 74504 | tf_op jit(solution)/shard_map/ppermute | solution.py:22
  53.1 6.8 %collective-permute-start.7 = (bf16[3,1,32,16]{3,2,1,0:T(8,128)(2,1)S(1)}, bf16[3,1,32,16]{3,2,1,0:T(8,128)(2,1)S(1)}, u32[]{:S(2)}, u32[]{:S(2)}) collective-permute-start(bf16[3,1,32,16]{3,2,1,0:T(8,128)(2,1)S(1)} %get-tuple-element.84), channel_id=1, source_target_pairs={{0,4},{1,5},{2,6},{3,7},{8,12},{9,13},{10,14},{11,15},{16,20},{17,... | collective-permute-start | bytes 9224 | tf_op jit(solution)/shard_map/ppermute | solution.py:42
  57.2 4.6 %collective-permute-start.8 = (bf16[3,1,32,16]{3,2,1,0:T(8,128)(2,1)S(1)}, bf16[3,1,32,16]{3,2,1,0:T(8,128)(2,1)S(1)}, u32[]{:S(2)}, u32[]{:S(2)}) collective-permute-start(bf16[3,1,32,16]{3,2,1,0:T(8,128)(2,1)S(1)} %get-tuple-element.85), channel_id=1, source_target_pairs={{4,0},{5,1},{6,2},{7,3},{12,8},{13,9},{14,10},{15,11},{20,16},{21,... | collective-permute-start | bytes 9224 | tf_op jit(solution)/shard_map/ppermute | solution.py:43
  61.7 0.8 copy-start.10
  62.5 16.2 %collective-permute-start.10 = (bf16[3,18,1,16]{3,2,1,0:T(2,128)(2,1)}, bf16[3,18,1,16]{3,2,1,0:T(2,128)(2,1)}, u32[]{:S(2)}, u32[]{:S(2)}) collective-permute-start(bf16[3,18,1,16]{3,2,1,0:T(2,128)(2,1)} %get-tuple-element.68), channel_id=1, source_target_pairs={{1,0},{2,1},{3,2},{5,4},{6,5},{7,6},{9,8},{10,9},{11,10},{13,12},{... | collective-permute-start | bytes 5192 | tf_op jit(solution)/shard_map/ppermute | solution.py:43
  72.9 8.1 %collective-permute-start.9 = (bf16[3,18,1,16]{3,2,1,0:T(2,128)(2,1)}, bf16[3,18,1,16]{3,2,1,0:T(2,128)(2,1)}, u32[]{:S(2)}, u32[]{:S(2)}) collective-permute-start(bf16[3,18,1,16]{3,2,1,0:T(2,128)(2,1)} %get-tuple-element.69), channel_id=1, source_target_pairs={{0,1},{1,2},{2,3},{4,5},{5,6},{6,7},{8,9},{9,10},{10,11},{12,13},{... | collective-permute-start | bytes 5192 | tf_op jit(solution)/shard_map/ppermute | solution.py:42
  83.3 2.2 %copy-start.15 = (bf16[512,16]{0,1:T(8,128)(2,1)S(1)}, bf16[512,16]{0,1:T(8,128)(2,1)}, u32[]{:S(2)}) copy-start(bf16[512,16]{0,1:T(8,128)(2,1)} %copy.41) | copy-start | bytes 49156
  83.3 2.8 %copy-start.16 = (bf16[512,16]{0,1:T(8,128)(2,1)S(1)}, bf16[512,16]{0,1:T(8,128)(2,1)}, u32[]{:S(2)}) copy-start(bf16[512,16]{0,1:T(8,128)(2,1)} %concatenate.149) | copy-start | bytes 49156
  83.4 3.9 %copy-start.14 = (bf16[512,16]{0,1:T(8,128)(2,1)S(1)}, bf16[512,16]{0,1:T(8,128)(2,1)}, u32[]{:S(2)}) copy-start(bf16[512,16]{0,1:T(8,128)(2,1)} %copy.42) | copy-start | bytes 49156
  83.4 5.7 %copy-start.13 = (bf16[512,16]{0,1:T(8,128)(2,1)S(1)}, bf16[512,16]{0,1:T(8,128)(2,1)}, u32[]{:S(2)}) copy-start(bf16[512,16]{0,1:T(8,128)(2,1)} %copy.43) | copy-start | bytes 49156
  83.9 17.4 %copy-start.22 = (f32[384]{0:T(512)S(1)}, f32[384]{0:T(512)}, u32[]{:S(2)}) copy-start(f32[384]{0:T(512)} %param.18) | copy-start | bytes 4612
  85.2 17.8 %copy-start.19 = (f32[384]{0:T(512)S(1)}, f32[384]{0:T(512)}, u32[]{:S(2)}) copy-start(f32[384]{0:T(512)} %param.19) | copy-start | bytes 4612
  101.3 17.6 %slice-start = ((s8[7962624]{0:T(1024)(128)(4,1)}), s8[4194304]{0:T(1024)(128)(4,1)S(1)}, s32[]{:S(2)}) async-start(s8[7962624]{0:T(1024)(128)(4,1)} %bitcast.198), calls=%async_computation | async-start | bytes 8388608
  103.4 4.0 %collective-permute-start.11 = (bf16[3,1,32,384]{3,2,1,0:T(8,128)(2,1)S(1)}, bf16[3,1,32,384]{3,2,1,0:T(8,128)(2,1)S(1)}, u32[]{:S(2)}, u32[]{:S(2)}) collective-permute-start(bf16[3,1,32,384]{3,2,1,0:T(8,128)(2,1)S(1)} %get-tuple-element.45), channel_id=1, source_target_pairs={{0,4},{1,5},{2,6},{3,7},{8,12},{9,13},{10,14},{11,15},{16,20},{17,... | collective-permute-start | bytes 221192 | tf_op jit(solution)/shard_map/ppermute | solution.py:42
  104.7 5.1 %collective-permute-start.12 = (bf16[3,1,32,384]{3,2,1,0:T(8,128)(2,1)S(1)}, bf16[3,1,32,384]{3,2,1,0:T(8,128)(2,1)S(1)}, u32[]{:S(2)}, u32[]{:S(2)}) collective-permute-start(bf16[3,1,32,384]{3,2,1,0:T(8,128)(2,1)S(1)} %get-tuple-element.46), channel_id=1, source_target_pairs={{4,0},{5,1},{6,2},{7,3},{12,8},{13,9},{14,10},{15,11},{20,16},{21,... | collective-permute-start | bytes 221192 | tf_op jit(solution)/shard_map/ppermute | solution.py:43
  107.4 11.5 %slice-start.1 = ((s8[7962624]{0:T(1024)(128)(4,1)}), s8[3768320]{0:T(1024)(128)(4,1)S(1)}, s32[]{:S(2)}) async-start(s8[7962624]{0:T(1024)(128)(4,1)} %bitcast.198), calls=%async_computation.1 | async-start | bytes 7536640
  111.7 10.0 %collective-permute-start.13 = (bf16[3,18,1,384]{3,2,1,0:T(2,128)(2,1)S(1)}, bf16[3,18,1,384]{3,2,1,0:T(2,128)(2,1)S(1)}, u32[]{:S(2)}, u32[]{:S(2)}) collective-permute-start(bf16[3,18,1,384]{3,2,1,0:T(2,128)(2,1)S(1)} %get-tuple-element.34), channel_id=1, source_target_pairs={{0,1},{1,2},{2,3},{4,5},{5,6},{6,7},{8,9},{9,10},{10,11},{12,13},{... | collective-permute-start | bytes 124424 | tf_op jit(solution)/shard_map/ppermute | solution.py:42
  113.7 8.0 %collective-permute-start.14 = (bf16[3,18,1,384]{3,2,1,0:T(2,128)(2,1)S(1)}, bf16[3,18,1,384]{3,2,1,0:T(2,128)(2,1)S(1)}, u32[]{:S(2)}, u32[]{:S(2)}) collective-permute-start(bf16[3,18,1,384]{3,2,1,0:T(2,128)(2,1)S(1)} %get-tuple-element.35), channel_id=1, source_target_pairs={{1,0},{2,1},{3,2},{5,4},{6,5},{7,6},{9,8},{10,9},{11,10},{13,12},{... | collective-permute-start | bytes 124424 | tf_op jit(solution)/shard_map/ppermute | solution.py:43
  129.3 1.0 copy-start.8
  129.8 1.0 copy-start.7
  130.2 1.1 copy-start.6
  130.7 1.0 copy-start.5
  131.8 1.0 copy-start.3
  133.5 1.1 copy-start.2
  133.5 1.2 copy-start.4
  133.6 1.2 copy-start.20
  134.8 12.6 %copy-start.12 = (f32[16,32]{1,0:T(8,128)S(1)}, f32[16,32]{1,0:T(8,128)}, u32[]{:S(2)}) copy-start(f32[16,32]{1,0:T(8,128)} %copy-done.11) | copy-start | bytes 6148
  135.4 2.7 %collective-permute-start.15 = (bf16[1,32,384]{2,1,0:T(8,128)(2,1)S(1)}, bf16[1,32,384]{2,1,0:T(8,128)(2,1)S(1)}, u32[]{:S(2)}, u32[]{:S(2)}) collective-permute-start(bf16[1,32,384]{2,1,0:T(8,128)(2,1)S(1)} %get-tuple-element.76), channel_id=1, source_target_pairs={{0,4},{1,5},{2,6},{3,7},{8,12},{9,13},{10,14},{11,15},{16,20},{17,... | collective-permute-start | bytes 73736 | tf_op jit(solution)/shard_map/ppermute | solution.py:42
  136.8 5.0 %collective-permute-start.16 = (bf16[1,32,384]{2,1,0:T(8,128)(2,1)S(1)}, bf16[1,32,384]{2,1,0:T(8,128)(2,1)S(1)}, u32[]{:S(2)}, u32[]{:S(2)}) collective-permute-start(bf16[1,32,384]{2,1,0:T(8,128)(2,1)S(1)} %get-tuple-element.77), channel_id=1, source_target_pairs={{4,0},{5,1},{6,2},{7,3},{12,8},{13,9},{14,10},{15,11},{20,16},{21,... | collective-permute-start | bytes 73736 | tf_op jit(solution)/shard_map/ppermute | solution.py:43
  141.9 6.0 %collective-permute-start.17 = (bf16[18,1,384]{2,1,0:T(2,128)(2,1)S(1)}, bf16[18,1,384]{2,1,0:T(2,128)(2,1)S(1)}, u32[]{:S(2)}, u32[]{:S(2)}) collective-permute-start(bf16[18,1,384]{2,1,0:T(2,128)(2,1)S(1)} %get-tuple-element.48), channel_id=1, source_target_pairs={{0,1},{1,2},{2,3},{4,5},{5,6},{6,7},{8,9},{9,10},{10,11},{12,13},{... | collective-permute-start | bytes 41480 | tf_op jit(solution)/shard_map/ppermute | solution.py:42
  145.2 5.2 %collective-permute-start.18 = (bf16[18,1,384]{2,1,0:T(2,128)(2,1)S(1)}, bf16[18,1,384]{2,1,0:T(2,128)(2,1)S(1)}, u32[]{:S(2)}, u32[]{:S(2)}) collective-permute-start(bf16[18,1,384]{2,1,0:T(2,128)(2,1)S(1)} %get-tuple-element.49), channel_id=1, source_target_pairs={{1,0},{2,1},{3,2},{5,4},{6,5},{7,6},{9,8},{10,9},{11,10},{13,12},{... | collective-permute-start | bytes 41480 | tf_op jit(solution)/shard_map/ppermute | solution.py:43
  158.1 3.6 %copy-start.9 = (bf16[3456,192]{0,1:T(8,128)(2,1)S(1)}, bf16[3456,192]{0,1:T(8,128)(2,1)}, u32[]{:S(2)}) copy-start(bf16[3456,192]{0,1:T(8,128)(2,1)} %param.22) | copy-start | bytes 3981316
  166.8 0.7 copy-start.21
  167.5 3.3 %copy-start.1 = (bf16[432,384]{1,0:T(8,128)(2,1)S(1)}, bf16[432,384]{1,0:T(8,128)(2,1)}, u32[]{:S(2)}) copy-start(bf16[432,384]{1,0:T(8,128)(2,1)} %param.17) | copy-start | bytes 995332
